TPU v7x, 32 devices: a whole 2x2x4 slice. The times are simulated.
32 devices in a mesh: req: 8 (over y, x, core), blk: 4 (over z).
Axes of the slice: x: 2, y: 2, z: 4, core: 2. Of those that a mesh axis runs over, the one named last changes fastest.
Arguments:
- x_img: bfloat16 [8, 1024, 1536], P('req', 'blk'), may hold values from -0.3 to 0.3
- x_txt: bfloat16 [8, 154, 1536], P('req'), may hold values from -6 to 6
- modulation: float32 [8, 7, 1536], P('req'), may hold values from -8 to 8
- w_img: bfloat16 [1536, 2304], P(None, 'req'), may hold values from -0.375 to 0.375
- w_txt: bfloat16 [1536, 1536], P(None, 'req'), may hold values from -0.15625 to 0.15625
- w_out: bfloat16 [768, 1536], P('req'), may hold values from -0.21875 to 0.21875
- w_final: bfloat16 [1536, 64], replicated, may hold values from -0.15625 to 0.15625
- lengths: int32 [8], P('req'), may hold values from 16 to 154, as said below
- block_mask: int32 [8, 4, 4], P('req', 'blk'), may hold values from 0 to 1, as said below
- timestep: int32 [8], P('req'), may hold values from 0 to 27
- latent: float32 [8, 16, 32, 128], P('req', None, 'blk'), may hold values from -6 to 6
- conv_w: bfloat16 [512, 144], replicated, may hold values from -0.5 to 0.5
Outputs:
- velocity: float32 [8, 16, 32, 128], P('req', None, 'blk')
- latent_next: float32 [8, 16, 32, 128], P('req', None, 'blk')
- features: bfloat16 [8, 512, 32, 128], P('req', None, 'blk')
Inputs may be any that keep to these rules, and one draw needn't show every extreme that they name: Text keys from position lengths[r] on are padding; some request uses all 154 text tokens. Every tile may attend to its own keys: block_mask[r, t, t] = 1.
All inputs are finite; a program needn't handle non-finite values.
Results may differ from a plain program's by a relative error of at most 0.0063.
Values may be sent and summed in bfloat16 or wider, within the bound.
A program may use at most 192 MiB of HBM per device.

v0:
```python
import jax
import jax.numpy as jnp
from jax import lax
from jax.sharding import PartitionSpec as P

HD = 64
GRIDW = 64
PATCH = 2
LATC = 16
NSTEPS = 28
NORM_EPS = 1e-06
SHIFT_FACTOR = 3.0
LATENT_SCALE = 1.5305
LATENT_SHIFT = 0.0609
NEG_LARGE = -1e30
SCORE_SCALE = 0.125


def with_halo(block, sides, width):
    for axis, dim in sides:
        count = lax.axis_size(axis)
        forward = [(i, i + 1) for i in range(count - 1)]
        backward = [(target, source) for source, target in forward]
        low = lax.ppermute(
            lax.slice_in_dim(block, block.shape[dim] - width, None, axis=dim), axis, forward
        )
        high = lax.ppermute(lax.slice_in_dim(block, 0, width, axis=dim), axis, backward)
        block = jnp.concatenate([low, block, high], axis=dim)
    return block


def layer_norm(values):
    values = values.astype(jnp.float32)
    center = values - jnp.mean(values, axis=-1, keepdims=True)
    spread = jnp.mean(center * center, axis=-1, keepdims=True)
    return center * lax.rsqrt(spread + NORM_EPS)


def modulate(values, shift_row, scale_row):
    return layer_norm(values) * (1.0 + scale_row) + shift_row


def sigma_of(step_index, step_count):
    fraction = 1.0 - step_index.astype(jnp.float32) / step_count
    return SHIFT_FACTOR * fraction / (1.0 + (SHIFT_FACTOR - 1.0) * fraction)


def unpatchify(token_out, grid_width, patch_size, channels):
    patch_rows = token_out.shape[0] // grid_width
    shaped = token_out.reshape(patch_rows, grid_width, patch_size, patch_size, channels)
    shaped = jnp.transpose(shaped, (4, 0, 2, 1, 3))
    return shaped.reshape(channels, patch_rows * patch_size, grid_width * patch_size)


def convolve(padded, conv_w):
    row_count = padded.shape[1] - 2
    col_count = padded.shape[2] - 2
    tap_list = [
        padded[:, tap_row : tap_row + row_count, tap_col : tap_col + col_count]
        for tap_row in range(3)
        for tap_col in range(3)
    ]
    stacked = jnp.stack(tap_list, axis=1).reshape(padded.shape[0] * 9, row_count * col_count)
    convolved = jnp.dot(conv_w, stacked, preferred_element_type=jnp.float32)
    return convolved.reshape(conv_w.shape[0], row_count, col_count)


def text_state(queries, keys_txt, vals_txt, length):
    text_allowed = (jnp.arange(keys_txt.shape[0], dtype=jnp.int32) < length)[None, None, :]
    text_scores = (
        jnp.einsum("qhd,khd->qhk", queries, keys_txt, preferred_element_type=jnp.float32)
        * SCORE_SCALE
    )
    text_scores = jnp.where(text_allowed, text_scores, NEG_LARGE)
    text_max = jnp.max(text_scores, axis=2)
    text_weights = jnp.where(text_allowed, jnp.exp(text_scores - text_max[:, :, None]), 0.0)
    text_acc = jnp.einsum(
        "qhk,khd->qhd",
        text_weights.astype(jnp.bfloat16),
        vals_txt,
        preferred_element_type=jnp.float32,
    )
    return (text_max, jnp.sum(text_weights, axis=2), text_acc)


def absorb_block(previous, queries, head_keys, head_vals, allowed):
    old_max, old_sum, old_acc = previous
    scores = (
        jnp.einsum("qhd,khd->qhk", queries, head_keys, preferred_element_type=jnp.float32)
        * SCORE_SCALE
    )
    scores = jnp.where(allowed, scores, NEG_LARGE)
    new_max = jnp.maximum(old_max, jnp.max(scores, axis=2))
    weights = jnp.where(allowed, jnp.exp(scores - new_max[:, :, None]), 0.0)
    factor = jnp.exp(old_max - new_max)
    summed = jnp.einsum(
        "qhk,khd->qhd", weights.astype(jnp.bfloat16), head_vals, preferred_element_type=jnp.float32
    )
    return (
        new_max,
        old_sum * factor + jnp.sum(weights, axis=2),
        old_acc * factor[:, :, None] + summed,
    )


def absorb_maybe(previous, queries, head_keys, head_vals, allowed):
    return absorb_block(previous, queries, head_keys, head_vals, allowed)


def on_device(
    x_img,
    x_txt,
    modulation,
    w_img,
    w_txt,
    w_out,
    w_final,
    lengths,
    block_mask,
    timestep,
    latent,
    conv_w,
):
    tokens = x_img[0]
    factors = modulation[0]
    tok_rows = tokens.shape[0]
    head_cols = w_out.shape[0] * lax.axis_size("req")
    head_count = head_cols // HD
    h_img = modulate(tokens, factors[0], factors[1]).astype(jnp.bfloat16)
    h_txt = modulate(x_txt[0], factors[3], factors[4]).astype(jnp.bfloat16)
    qkv = jnp.dot(
        h_img, lax.all_gather(w_img, "req", axis=1, tiled=True), preferred_element_type=jnp.float32
    ).astype(jnp.bfloat16)
    kv_txt = jnp.dot(
        h_txt, lax.all_gather(w_txt, "req", axis=1, tiled=True), preferred_element_type=jnp.float32
    ).astype(jnp.bfloat16)
    keys_txt = kv_txt[:, :head_cols].reshape(-1, head_count, HD)
    vals_txt = kv_txt[:, head_cols:].reshape(-1, head_count, HD)
    length = lengths[0]
    queries = qkv[:, :head_cols].reshape(tok_rows, head_count, HD)
    keys_img = qkv[:, head_cols : 2 * head_cols]
    vals_img = qkv[:, 2 * head_cols :]
    mask_row = block_mask[0, 0]
    tile_count = mask_row.shape[0]
    start_state = text_state(queries, keys_txt, vals_txt, length)
    piece_keys = lax.all_gather(keys_img, "blk", axis=0, tiled=True)
    piece_vals = lax.all_gather(vals_img, "blk", axis=0, tiled=True)
    piece_len = piece_keys.shape[0]
    key_tile = jnp.arange(piece_len, dtype=jnp.int32) // tok_rows
    tile_hit = key_tile[:, None] == jnp.arange(tile_count, dtype=jnp.int32)[None, :]
    allowed = jnp.sum(jnp.where(tile_hit, mask_row[None, :], 0), axis=1) == 1
    head_keys = piece_keys.reshape(piece_len, head_count, HD)
    head_vals = piece_vals.reshape(piece_len, head_count, HD)
    run_max, run_sum, run_acc = absorb_maybe(
        start_state, queries, head_keys, head_vals, allowed[None, None, :]
    )
    attended = (run_acc / run_sum[:, :, None]).reshape(tok_rows, head_cols).astype(jnp.bfloat16)
    projected = jnp.dot(
        attended,
        lax.all_gather(w_out, "req", axis=0, tiled=True),
        preferred_element_type=jnp.float32,
    )
    residual = tokens.astype(jnp.float32) + factors[2] * projected
    final_in = modulate(residual, factors[5], factors[6]).astype(jnp.bfloat16)
    token_out = jnp.dot(final_in, w_final, preferred_element_type=jnp.float32)
    velocity = unpatchify(token_out, GRIDW, PATCH, LATC)[None]
    step_index = timestep[0]
    sigma_step = sigma_of(step_index + 1, NSTEPS) - sigma_of(step_index, NSTEPS)
    latent_next = latent + sigma_step * velocity
    decoded = (latent_next / LATENT_SCALE + LATENT_SHIFT).astype(jnp.bfloat16)
    padded = with_halo(decoded, (("blk", 2),), 1)
    padded = jnp.pad(padded[0], ((0, 0), (0, 0), (1, 1)))
    features = convolve(padded, conv_w).astype(jnp.bfloat16)[None]
    return (velocity, latent_next, features)


def solution(mesh):
    return jax.shard_map(
        on_device,
        mesh=mesh,
        in_specs=(
            P("req", "blk", None),
            P("req", None, None),
            P("req", None, None),
            P(None, "req"),
            P(None, "req"),
            P("req", None),
            P(),
            P("req"),
            P("req", "blk", None),
            P("req"),
            P("req", None, "blk", None),
            P(),
        ),
        out_specs=(
            P("req", None, "blk", None),
            P("req", None, "blk", None),
            P("req", None, "blk", None),
        ),
        check_vma=False,
    )
```

profile of v0, /device:TPU:0, one launch (start us, length us, event | category | flops | bytes accessed | tf_op | source)
XLA Modules:
  0.0 230.1 jit_solution(16971153236048344387)
XLA Ops:
  8.7 0.9 add_reduce_fusion
  10.2 51.3 %all-gather.8.cloned.1.call-done = bf16[1536,2304]{0,1:T(8,128)(2,1)} async-done(((bf16[1536,288]{0,1:T(8,128)(2,1)}), bf16[1536,2304]{0,1:T(8,128)(2,1)}) %all-gather.8.cloned.1.call-update) | async-done | bytes 7077904 | tf_op jit(solution)/shard_map/all_gather | solution.py:132
  61.5 5.2 %convolution_convert_fusion = bf16[256,2304]{1,0:T(8,128)(2,1)S(1)} fusion(bf16[1536,2304]{0,1:T(8,128)(2,1)} %all-gather.8.cloned.1.call-done, bf16[1,256,1536]{2,1,0:T(8,128)(2,1)S(1)} %copy-done.2, f32[1536]{0:T(1024)S(1)} %get-tuple-element.16, f32[1536]{0:T(1024)S(1)} %get-tuple-element.17, f32[256]{0:T(256)S(1)} %add_rsqrt_fusion.1, ...), kind=kOutput, calls=%fused_computation.10 | convolution fusion | flops 1814888448 | bytes 9058304 | tf_op jit(solution)/shard_map/dot_general | solution.py:131
  66.7 1.0 fusion.69
  70.8 1.0 copy.66
  71.9 30.4 %all-gather.6.cloned.1.call-done = bf16[1536,1536]{0,1:T(8,128)(2,1)} async-done(((bf16[1536,192]{0,1:T(8,128)(2,1)}), bf16[1536,1536]{0,1:T(8,128)(2,1)}) %all-gather.6.cloned.1.call-update) | async-done | bytes 4718608 | tf_op jit(solution)/shard_map/all_gather | solution.py:135
  102.3 4.0 %convolution_convert_fusion.1 = bf16[154,1536]{1,0:T(8,128)(2,1)S(1)} fusion(bf16[1536,1536]{0,1:T(8,128)(2,1)} %all-gather.6.cloned.1.call-done, bf16[1,154,1536]{2,1,0:T(8,128)(2,1)S(1)} %copy-done.4, f32[1536]{0:T(1024)S(1)} %get-tuple-element.18, f32[1536]{0:T(1024)S(1)} %get-tuple-element.19, f32[154]{0:T(256)S(1)} %add_rsqrt_fusion.2, ...), kind=kOutput, calls=%fused_computation.13 | convolution fusion | flops 728318976 | bytes 5678288 | tf_op jit(solution)/shard_map/dot_general | solution.py:134
  106.4 0.9 copy.60
  107.3 0.9 copy.59
  108.4 1.6 bitcast_reduce_fusion.1
  110.6 30.5 %all-gather.10.cloned.1.call-done = bf16[1024,768]{1,0:T(8,128)(2,1)} async-done(((bf16[256,768]{1,0:T(8,128)(2,1)}), bf16[1024,768]{1,0:T(8,128)(2,1)}) %all-gather.10.cloned.1.call-update) | async-done | bytes 1572880 | tf_op jit(solution)/shard_map/all_gather | solution.py:146
  141.0 2.6 %copy.62 = bf16[1024,768]{0,1:T(8,128)(2,1)} copy(bf16[1024,768]{1,0:T(8,128)(2,1)} %all-gather.10.cloned.1.call-done) | data formatting | bytes 3145728 | tf_op jit(solution)/shard_map/all_gather | solution.py:146
  143.6 8.8 %bitcast_reduce_fusion = (f32[256,12]{0,1:T(8,128)S(1)}, f32[12,1024,256]{2,1,0:T(8,128)}) fusion(pred[1024]{0:T(1024)(128)(4,1)S(1)} %broadcast_compare_fusion, bf16[1024,12,64]{0,2,1:T(8,128)(2,1)} %bitcast.129, bf16[256,12,64]{0,2,1:T(8,128)(2,1)S(1)} %bitcast.134), kind=kOutput, calls=%fused_computation.1 | convolution fusion | flops 412087296 | bytes 14562304 | tf_op jit(solution)/shard_map/qhd,khd->qhk/dot_general | solution.py:89
  152.5 26.0 %all-gather.12.cloned.1.call-done = bf16[1024,768]{1,0:T(8,128)(2,1)} async-done(((bf16[256,768]{1,0:T(8,128)(2,1)}), bf16[1024,768]{1,0:T(8,128)(2,1)}) %all-gather.12.cloned.1.call-update) | async-done | bytes 1572880 | tf_op jit(solution)/shard_map/all_gather | solution.py:147
  178.4 2.6 %copy.63 = bf16[1024,768]{0,1:T(8,128)(2,1)} copy(bf16[1024,768]{1,0:T(8,128)(2,1)} %all-gather.12.cloned.1.call-done) | data formatting | bytes 3145728 | tf_op jit(solution)/shard_map/all_gather | solution.py:147
  181.0 7.2 %fusion.2 = f32[256,12]{0,1:T(8,128)S(1)} fusion(f32[12,1024,256]{2,1,0:T(8,128)} %get-tuple-element.45, f32[256,12]{0,1:T(8,128)S(1)} %max.13, pred[1024]{0:T(1024)(128)(4,1)S(1)} %broadcast_compare_fusion), kind=kLoop, calls=%fused_computation.5 | loop fusion | flops 15725568 | bytes 12608512 | tf_op jit(solution)/shard_map/reduce_sum | solution.py:101
  188.3 1.3 copy-done.1
  189.6 4.3 %fusion.20 = f32[256,12,64]{0,2,1:T(8,128)S(1)} fusion(bf16[1024,12,64]{0,2,1:T(8,128)(2,1)} %bitcast.135, f32[12,1024,256]{2,1,0:T(8,128)S(1)} %copy-done.1, f32[256,12]{0,1:T(8,128)S(1)} %max.13, pred[1024]{0:T(1024)(128)(4,1)S(1)} %broadcast_compare_fusion), kind=kOutput, calls=%fused_computation.33 | convolution fusion | flops 418381824 | bytes 14955520 | tf_op jit(solution)/shard_map/qhk,khd->qhd/dot_general | solution.py:96
  194.6 13.5 %all-gather.14.cloned.1.call-done = bf16[768,1536]{1,0:T(8,128)(2,1)} async-done(((bf16[96,1536]{1,0:T(8,128)(2,1)}), bf16[768,1536]{1,0:T(8,128)(2,1)}) %all-gather.14.cloned.1.call-update) | async-done | bytes 2359312 | tf_op jit(solution)/shard_map/all_gather | solution.py:160
  208.1 2.5 %fusion.72 = (f32[256]{0:T(256)S(1)}, f32[256,1536]{1,0:T(8,128)S(1)}) fusion(bf16[256,768]{0,1:T(8,128)(2,1)S(1)} %bitcast.137, bf16[768,1536]{1,0:T(8,128)(2,1)} %all-gather.14.cloned.1.call-done, f32[1536]{0:T(1024)S(1)} %get-tuple-element.20, bf16[1,256,1536]{2,1,0:T(8,128)(2,1)S(1)} %copy-done.2), kind=kOutput, calls=%fused_computation.127 | convolution fusion | flops 605552384 | bytes 5118976 | tf_op jit(solution)/shard_map/dot_general | solution.py:158
  212.0 3.4 %collective-permute-start = (bf16[1,16,1,128]{1,3,2,0:T(8,128)(2,1)S(1)}, bf16[1,16,1,128]{1,3,2,0:T(8,128)(2,1)S(1)}, u32[]{:S(2)}, u32[]{:S(2)}) collective-permute-start(bf16[1,16,1,128]{1,3,2,0:T(8,128)(2,1)S(1)} %get-tuple-element.31), channel_id=1, source_target_pairs={{0,1},{1,2},{2,3},{4,5},{5,6},{6,7},{8,9},{9,10},{10,11},{12,13},{... | collective-permute-start | bytes 12296 | tf_op jit(solution)/shard_map/ppermute | solution.py:24
  215.4 1.3 collective-permute-start.1
  218.5 2.7 %collective-permute-done.1 = bf16[1,16,1,128]{1,3,2,0:T(8,128)(2,1)S(1)} collective-permute-done((bf16[1,16,1,128]{1,3,2,0:T(8,128)(2,1)S(1)}, bf16[1,16,1,128]{1,3,2,0:T(8,128)(2,1)S(1)}, u32[]{:S(2)}, u32[]{:S(2)}) %collective-permute-start.1) | collective-permute-done | bytes 4128 | tf_op jit(solution)/shard_map/ppermute | solution.py:27
  222.1 1.5 copy.81
  (71 shorter events, 9.1 us)
Async XLA Ops:
  7.2 203.8 %copy-start = (bf16[1536,64]{0,1:T(8,128)(2,1)S(1)}, bf16[1536,64]{0,1:T(8,128)(2,1)}, u32[]{:S(2)}) copy-start(bf16[1536,64]{0,1:T(8,128)(2,1)} %param.18) | copy-start | bytes 589828
  7.2 2.5 %copy-start.2 = (bf16[1,256,1536]{2,1,0:T(8,128)(2,1)S(1)}, bf16[1,256,1536]{2,1,0:T(8,128)(2,1)}, u32[]{:S(2)}) copy-start(bf16[1,256,1536]{2,1,0:T(8,128)(2,1)} %param.12) | copy-start | bytes 2359300
  7.2 54.3 %all-gather.8.cloned.1.call-start = ((), (), s32[]{:S(2)}) async-start(), calls=%async_computation.1 | async-start | bytes 7962624 | tf_op jit(solution)/shard_map/all_gather | solution.py:132
  7.9 94.4 %all-gather.6.cloned.1.call-start = ((), (), s32[]{:S(2)}) async-start(), calls=%async_computation | async-start | bytes 5308416 | tf_op jit(solution)/shard_map/all_gather | solution.py:135
  8.7 132.4 %all-gather.10.cloned.1.call-start = ((), (), s32[]{:S(2)}) async-start(), calls=%async_computation.2 | async-start | bytes 1966080 | tf_op jit(solution)/shard_map/all_gather | solution.py:146
  66.7 2.9 %copy-start.4 = (bf16[1,154,1536]{2,1,0:T(8,128)(2,1)S(1)}, bf16[1,154,1536]{2,1,0:T(8,128)(2,1)}, u32[]{:S(2)}) copy-start(bf16[1,154,1536]{2,1,0:T(8,128)(2,1)} %param.13) | copy-start | bytes 1419268
  66.7 4.0 %copy-start.8 = (s32[1,1,4]{2,1,0:T(1,128)S(1)}, s32[1,1,4]{2,1,0:T(1,128)}, u32[]{:S(2)}) copy-start(s32[1,1,4]{2,1,0:T(1,128)} %param.20) | copy-start | bytes 52
  66.7 4.1 %copy-start.7 = (f32[1,16,8,128]{3,2,1,0:T(8,128)S(1)}, f32[1,16,8,128]{3,2,1,0:T(8,128)}, u32[]{:S(2)}) copy-start(f32[1,16,8,128]{3,2,1,0:T(8,128)} %param.22) | copy-start | bytes 196612
  67.7 110.8 %all-gather.12.cloned.1.call-start = ((), (), s32[]{:S(2)}) async-start(), calls=%async_computation.3 | async-start | bytes 1966080 | tf_op jit(solution)/shard_map/all_gather | solution.py:147
  68.3 139.8 %all-gather.14.cloned.1.call-start = ((), (), s32[]{:S(2)}) async-start(), calls=%async_computation.4 | async-start | bytes 2654208 | tf_op jit(solution)/shard_map/all_gather | solution.py:160
  181.0 8.5 %copy-start.1 = (f32[12,1024,256]{2,1,0:T(8,128)S(1)}, f32[12,1024,256]{2,1,0:T(8,128)}, u32[]{:S(2)}) copy-start(f32[12,1024,256]{2,1,0:T(8,128)} %get-tuple-element.45) | copy-start | bytes 37748740
  189.6 4.3 %copy-start.5 = (bf16[154,768]{0,1:T(8,128)(2,1)S(1)}, bf16[154,768]{0,1:T(8,128)(2,1)}, u32[]{:S(2)}) copy-start(bf16[154,768]{0,1:T(8,128)(2,1)} %copy.59) | copy-start | bytes 709636
  210.6 1.2 copy-start.3
  211.8 9.8 %copy-start.6 = (bf16[512,144]{0,1:T(8,128)(2,1)S(1)}, bf16[512,144]{0,1:T(8,128)(2,1)}, u32[]{:S(2)}) copy-start(bf16[512,144]{0,1:T(8,128)(2,1)} %param.23) | copy-start | bytes 442372
  212.0 6.4 %collective-permute-start = (bf16[1,16,1,128]{1,3,2,0:T(8,128)(2,1)S(1)}, bf16[1,16,1,128]{1,3,2,0:T(8,128)(2,1)S(1)}, u32[]{:S(2)}, u32[]{:S(2)}) collective-permute-start(bf16[1,16,1,128]{1,3,2,0:T(8,128)(2,1)S(1)} %get-tuple-element.31), channel_id=1, source_target_pairs={{0,1},{1,2},{2,3},{4,5},{5,6},{6,7},{8,9},{9,10},{10,11},{12,13},{... | collective-permute-start | bytes 12296 | tf_op jit(solution)/shard_map/ppermute | solution.py:24
  215.4 5.8 %collective-permute-start.1 = (bf16[1,16,1,128]{1,3,2,0:T(8,128)(2,1)S(1)}, bf16[1,16,1,128]{1,3,2,0:T(8,128)(2,1)S(1)}, u32[]{:S(2)}, u32[]{:S(2)}) collective-permute-start(bf16[1,16,1,128]{1,3,2,0:T(8,128)(2,1)S(1)} %get-tuple-element.32), channel_id=1, source_target_pairs={{1,0},{2,1},{3,2},{5,4},{6,5},{7,6},{9,8},{10,9},{11,10},{13,12},{... | collective-permute-start | bytes 12296 | tf_op jit(solution)/shard_map/ppermute | solution.py:27
Sparse Core Ops, SparseCore 0:
  9.9 51.5 all-gather.7
  63.4 38.9 all-gather.5
  103.9 37.0 all-gather.9
  142.5 35.9 all-gather.11
  180.2 27.8 all-gather.13
where the time goes:
time: 231 us; the launch traced here: 230 us
  waiting for transfers between devices  157 us (68%)
  matrix products  28 us (12%)
  between operations  15.5 us (7%)
  local copies, waits for them, and re-layouts  14.5 us (6%)
  other arithmetic  10.2 us (4%)
  starting transfers between devices  4.88 us (2%)
    all_gather x1, waiting for transfers between devices, on_device(): lax.all_gather(w_img, 'req', axis=1, tiled=True)  51.3 us
    all_gather x1, waiting for transfers between devices, on_device(): piece_keys = lax.all_gather(keys_img, 'blk', axis=0, tiled=True)  30.5 us
    all_gather x1, waiting for transfers between devices, on_device(): lax.all_gather(w_txt, 'req', axis=1, tiled=True)  30.4 us
    all_gather x1, waiting for transfers between devices, on_device(): piece_vals = lax.all_gather(vals_img, 'blk', axis=0, tiled=True)  26 us
    all_gather x1, waiting for transfers between devices, on_device(): lax.all_gather(w_out, 'req', axis=0, tiled=True)  13.5 us
    dot_general x1, matrix products, absorb_block(): jnp.einsum('qhd,khd->qhk', queries, head_keys, preferred_element_type=jnp...  8.82 us
    reduce_sum x1, other arithmetic, absorb_block(): jnp.sum(weights, axis=2)  7.21 us
    unnamed x30, local copies, waits for them, and re-layouts  5.57 us
  transfers between devices with their start and end apart: 7, of which 6 were waited for; matrix products, arithmetic and copies ran while one was open for 20% of the time, Pallas kernels for 0%

commit v1 on v0

--- a/solution.py
+++ b/solution.py
@@ -143,7 +143,26 @@
     mask_row = block_mask[0, 0]
     tile_count = mask_row.shape[0]
     start_state = text_state(queries, keys_txt, vals_txt, length)
-    piece_keys = lax.all_gather(keys_img, "blk", axis=0, tiled=True)
+    devices, index, rows = (lax.axis_size("blk"), lax.axis_index("blk"), keys_img.shape[0])
+    right = [(i_2, (i_2 + 1) % devices) for i_2 in range(devices)]
+    backward_2 = [(i_2, (i_2 - 1) % devices) for i_2 in range(devices)]
+    filled = jnp.zeros(
+        (*keys_img.shape[:0], devices * rows, *keys_img.shape[0 + 1 :]), keys_img.dtype
+    )
+    filled = lax.dynamic_update_slice_in_dim(filled, keys_img, index * rows, axis=0)
+    from_left = from_right = keys_img
+    half = devices // 2
+    for turn in range(1, half + 1):
+        from_left = lax.ppermute(from_left, "blk", right)
+        filled = lax.dynamic_update_slice_in_dim(
+            filled, from_left, (index - turn) % devices * rows, axis=0
+        )
+        if turn < devices - half:
+            from_right = lax.ppermute(from_right, "blk", backward_2)
+            filled = lax.dynamic_update_slice_in_dim(
+                filled, from_right, (index + turn) % devices * rows, axis=0
+            )
+    piece_keys = filled
     piece_vals = lax.all_gather(vals_img, "blk", axis=0, tiled=True)
     piece_len = piece_keys.shape[0]
     key_tile = jnp.arange(piece_len, dtype=jnp.int32) // tok_rows

time: 231 us -> 214 us (0.926)
  waiting for transfers between devices: 157 us -> 118 us
  starting transfers between devices: 4.88 us -> 18.3 us
  local copies, waits for them, and re-layouts: 14.5 us -> 27.9 us
  other arithmetic: 10.2 us -> 6.59 us
    all_gather x1 -> x0, waiting for transfers between devices: 30.5 us -> none  [on_device(): piece_keys = lax.all_gather(keys_img, 'blk', axis=0, tiled=True)]
    all_gather x1, waiting for transfers between devices: 26 us -> 0.02 us  [on_device(): piece_vals = lax.all_gather(vals_img, 'blk', axis=0, tiled=True)]
    ppermute x0 -> x3, waiting for transfers between devices: none -> 21.2 us  [the longest x2 13.4 us: on_device(): from_left = lax.ppermute(from_left, 'blk', right)]
    ppermute x0 -> x3, starting transfers between devices: none -> 13.5 us  [the longest x2 11.2 us: on_device(): from_left = lax.ppermute(from_left, 'blk', right)]
    dynamic_update_slice x0 -> x4, local copies, waits for them, and re-layouts: none -> 7.21 us  [the longest x2 3.61 us: on_device(): lax.dynamic_update_slice_in_dim(filled, from_left, (index - turn) % devic...]
    ppermute x0 -> x3, local copies, waits for them, and re-layouts: none -> 5.78 us  [the longest x2 3.85 us: on_device(): from_left = lax.ppermute(from_left, 'blk', right)]
    dot_general x1, matrix products: 8.82 us -> 4.23 us  [absorb_block(): jnp.einsum('qhd,khd->qhk', queries, head_keys, preferred_element_type=jnp...]
    all_gather x1, waiting for transfers between devices: 13.5 us -> 9.37 us  [on_device(): lax.all_gather(w_out, 'req', axis=0, tiled=True)]
  transfers between devices with their start and end apart: 7 -> 9, of which waited for: 6 -> 7; matrix products, arithmetic and copies ran while one was open for 20% -> 26% of each run, Pallas kernels for 0% -> 0%
where the time goes in v1:
time: 214 us; the launch traced here: 213 us
  waiting for transfers between devices  118 us (55%)
  local copies, waits for them, and re-layouts  27.9 us (13%)
  matrix products  27 us (13%)
  starting transfers between devices  18.3 us (9%)
  between operations  15.6 us (7%)
  other arithmetic  6.59 us (3%)
    all_gather x1, waiting for transfers between devices, on_device(): lax.all_gather(w_img, 'req', axis=1, tiled=True)  51.3 us
    all_gather x1, waiting for transfers between devices, on_device(): lax.all_gather(w_txt, 'req', axis=1, tiled=True)  31 us
    ppermute x2, waiting for transfers between devices, on_device(): from_left = lax.ppermute(from_left, 'blk', right)  13.4 us
    ppermute x2, starting transfers between devices, on_device(): from_left = lax.ppermute(from_left, 'blk', right)  11.2 us
    all_gather x1, waiting for transfers between devices, on_device(): lax.all_gather(w_out, 'req', axis=0, tiled=True)  9.37 us
    dot_general x1, matrix products, absorb_block(): jnp.einsum('qhk,khd->qhd', weights.astype(jnp.bfloat16), head_vals, prefe...  7.82 us
    ppermute x1, waiting for transfers between devices, on_device(): from_right = lax.ppermute(from_right, 'blk', backward_2)  7.78 us
    unnamed x30, local copies, waits for them, and re-layouts  5.23 us
  transfers between devices with their start and end apart: 9, of which 7 were waited for; matrix products, arithmetic and copies ran while one was open for 26% of the time, Pallas kernels for 0%

profile of v1, /device:TPU:0, one launch (start us, length us, event | category | flops | bytes accessed | tf_op | source)
XLA Modules:
  0.0 213.0 jit_solution(4402754046131051732)
XLA Ops:
  10.2 51.3 %all-gather.7.cloned.1.call-done = bf16[1536,2304]{0,1:T(8,128)(2,1)} async-done(((bf16[1536,288]{0,1:T(8,128)(2,1)}), bf16[1536,2304]{0,1:T(8,128)(2,1)}) %all-gather.7.cloned.1.call-update) | async-done | bytes 7077904 | tf_op jit(solution)/shard_map/all_gather | solution.py:132
  61.5 5.2 %convolution_convert_fusion = bf16[256,2304]{1,0:T(8,128)(2,1)S(1)} fusion(bf16[1536,2304]{0,1:T(8,128)(2,1)} %all-gather.7.cloned.1.call-done, bf16[1,256,1536]{2,1,0:T(8,128)(2,1)S(1)} %copy-done.2, f32[1536]{0:T(1024)S(1)} %get-tuple-element.16, f32[1536]{0:T(1024)S(1)} %get-tuple-element.17, f32[256]{0:T(256)S(1)} %add_rsqrt_fusion.1, ...), kind=kOutput, calls=%fused_computation.10 | convolution fusion | flops 1814888448 | bytes 9058304 | tf_op jit(solution)/shard_map/dot_general | solution.py:131
  71.4 31.0 %all-gather.5.cloned.1.call-done = bf16[1536,1536]{0,1:T(8,128)(2,1)} async-done(((bf16[1536,192]{0,1:T(8,128)(2,1)}), bf16[1536,1536]{0,1:T(8,128)(2,1)}) %all-gather.5.cloned.1.call-update) | async-done | bytes 4718608 | tf_op jit(solution)/shard_map/all_gather | solution.py:135
  102.3 4.0 %convolution_convert_fusion.1 = bf16[154,1536]{1,0:T(8,128)(2,1)S(1)} fusion(bf16[1536,1536]{0,1:T(8,128)(2,1)} %all-gather.5.cloned.1.call-done, bf16[1,154,1536]{2,1,0:T(8,128)(2,1)S(1)} %copy-done.4, f32[1536]{0:T(1024)S(1)} %get-tuple-element.18, f32[1536]{0:T(1024)S(1)} %get-tuple-element.19, f32[154]{0:T(256)S(1)} %add_rsqrt_fusion.2, ...), kind=kOutput, calls=%fused_computation.13 | convolution fusion | flops 728318976 | bytes 5678288 | tf_op jit(solution)/shard_map/dot_general | solution.py:134
  109.8 2.3 %collective-permute-start.1 = (bf16[256,768]{1,0:T(8,128)(2,1)}, bf16[256,768]{1,0:T(8,128)(2,1)}, u32[]{:S(2)}, u32[]{:S(2)}) collective-permute-start(bf16[256,768]{1,0:T(8,128)(2,1)} %get-tuple-element.28), channel_id=1, source_target_pairs={{0,3},{1,0},{2,1},{3,2},{4,7},{5,4},{6,5},{7,6},{8,11},{9,8},{10,9... | collective-permute-start | bytes 1179656 | tf_op jit(solution)/shard_map/ppermute | solution.py:161
  113.9 10.9 %collective-permute-done = bf16[256,768]{1,0:T(8,128)(2,1)} collective-permute-done((bf16[256,768]{1,0:T(8,128)(2,1)}, bf16[256,768]{1,0:T(8,128)(2,1)}, u32[]{:S(2)}, u32[]{:S(2)}) %collective-permute-start) | collective-permute-done | bytes 393248 | tf_op jit(solution)/shard_map/ppermute | solution.py:156
  124.8 9.6 %collective-permute-start.2 = (bf16[256,768]{1,0:T(8,128)(2,1)}, bf16[256,768]{1,0:T(8,128)(2,1)}, u32[]{:S(2)}, u32[]{:S(2)}) collective-permute-start(bf16[256,768]{1,0:T(8,128)(2,1)} %collective-permute-done), channel_id=1, source_target_pairs={{0,1},{1,2},{2,3},{3,0},{4,5},{5,6},{6,7},{7,4},{8,9},{9,10},{10,1... | collective-permute-start | bytes 1179656 | tf_op jit(solution)/shard_map/ppermute | solution.py:156
  134.9 1.9 copy.71
  138.2 1.8 constant_dynamic-update-slice_fusion.2
  140.0 1.9 copy.72
  142.0 7.8 %collective-permute-done.1 = bf16[256,768]{1,0:T(8,128)(2,1)} collective-permute-done((bf16[256,768]{1,0:T(8,128)(2,1)}, bf16[256,768]{1,0:T(8,128)(2,1)}, u32[]{:S(2)}, u32[]{:S(2)}) %collective-permute-start.1) | collective-permute-done | bytes 393248 | tf_op jit(solution)/shard_map/ppermute | solution.py:161
  149.8 1.9 copy.73
  153.5 1.8 constant_dynamic-update-slice_fusion
  155.3 2.6 %collective-permute-done.2 = bf16[256,768]{1,0:T(8,128)(2,1)} collective-permute-done((bf16[256,768]{1,0:T(8,128)(2,1)}, bf16[256,768]{1,0:T(8,128)(2,1)}, u32[]{:S(2)}, u32[]{:S(2)}) %collective-permute-start.2) | collective-permute-done | bytes 393248 | tf_op jit(solution)/shard_map/ppermute | solution.py:156
  157.9 1.9 copy.74
  159.8 1.8 constant_dynamic-update-slice_fusion.3
  161.6 4.2 %bitcast_reduce_fusion = (f32[256,12]{0,1:T(8,128)S(1)}, f32[12,1024,256]{2,1,0:T(8,128)S(1)}) fusion(pred[1024]{0:T(1024)(128)(4,1)S(1)} %broadcast_compare_fusion, bf16[1024,12,64]{0,2,1:T(8,128)(2,1)} %bitcast.9, bf16[256,12,64]{0,2,1:T(8,128)(2,1)S(1)} %bitcast.133), kind=kOutput, calls=%fused_computation.1 | convolution fusion | flops 412087296 | bytes 14562304 | tf_op jit(solution)/shard_map/qhd,khd->qhk/dot_general | solution.py:89
  165.8 3.6 %fusion.2 = f32[256,12]{0,1:T(8,128)S(1)} fusion(f32[12,1024,256]{2,1,0:T(8,128)S(1)} %get-tuple-element.45, f32[256,12]{0,1:T(8,128)S(1)} %max.13, pred[1024]{0:T(1024)(128)(4,1)S(1)} %broadcast_compare_fusion), kind=kLoop, calls=%fused_computation.5 | loop fusion | flops 15725568 | bytes 12608512 | tf_op jit(solution)/shard_map/reduce_sum | solution.py:101
  170.4 2.6 %copy.75 = bf16[1024,768]{0,1:T(8,128)(2,1)} copy(bf16[1024,768]{1,0:T(8,128)(2,1)} %all-gather.9.cloned.1.call-done) | data formatting | bytes 3145728 | tf_op jit(solution)/shard_map/all_gather | solution.py:166
  173.0 7.8 %fusion.20 = f32[256,12,64]{0,2,1:T(8,128)S(1)} fusion(bf16[1024,12,64]{0,2,1:T(8,128)(2,1)} %bitcast.134, f32[12,1024,256]{2,1,0:T(8,128)} %copy-done.1, f32[256,12]{0,1:T(8,128)S(1)} %max.13, pred[1024]{0:T(1024)(128)(4,1)S(1)} %broadcast_compare_fusion), kind=kOutput, calls=%fused_computation.33 | convolution fusion | flops 418381824 | bytes 14955520 | tf_op jit(solution)/shard_map/qhk,khd->qhd/dot_general | solution.py:96
  181.5 9.4 %all-gather.11.cloned.1.call-done = bf16[768,1536]{1,0:T(8,128)(2,1)} async-done(((bf16[96,1536]{1,0:T(8,128)(2,1)}), bf16[768,1536]{1,0:T(8,128)(2,1)}) %all-gather.11.cloned.1.call-update) | async-done | bytes 2359312 | tf_op jit(solution)/shard_map/all_gather | solution.py:179
  190.9 2.5 %fusion.72 = (f32[256]{0:T(256)S(1)}, f32[256,1536]{1,0:T(8,128)S(1)}) fusion(bf16[256,768]{0,1:T(8,128)(2,1)S(1)} %bitcast.136, bf16[768,1536]{1,0:T(8,128)(2,1)} %all-gather.11.cloned.1.call-done, f32[1536]{0:T(1024)S(1)} %get-tuple-element.20, bf16[1,256,1536]{2,1,0:T(8,128)(2,1)S(1)} %copy-done.2), kind=kOutput, calls=%fused_computation.131 | convolution fusion | flops 605552384 | bytes 5118976 | tf_op jit(solution)/shard_map/dot_general | solution.py:177
  194.8 3.4 %collective-permute-start.3 = (bf16[1,16,1,128]{1,3,2,0:T(8,128)(2,1)S(1)}, bf16[1,16,1,128]{1,3,2,0:T(8,128)(2,1)S(1)}, u32[]{:S(2)}, u32[]{:S(2)}) collective-permute-start(bf16[1,16,1,128]{1,3,2,0:T(8,128)(2,1)S(1)} %get-tuple-element.31), channel_id=1, source_target_pairs={{0,1},{1,2},{2,3},{4,5},{5,6},{6,7},{8,9},{9,10},{10,11},{12,13},{... | collective-permute-start | bytes 12296 | tf_op jit(solution)/shard_map/ppermute | solution.py:24
  201.3 2.7 %collective-permute-done.4 = bf16[1,16,1,128]{1,3,2,0:T(8,128)(2,1)S(1)} collective-permute-done((bf16[1,16,1,128]{1,3,2,0:T(8,128)(2,1)S(1)}, bf16[1,16,1,128]{1,3,2,0:T(8,128)(2,1)S(1)}, u32[]{:S(2)}, u32[]{:S(2)}) %collective-permute-start.4) | collective-permute-done | bytes 4128 | tf_op jit(solution)/shard_map/ppermute | solution.py:27
  (82 shorter events, 23.3 us)
Async XLA Ops:
  7.2 186.6 %copy-start = (bf16[1536,64]{0,1:T(8,128)(2,1)S(1)}, bf16[1536,64]{0,1:T(8,128)(2,1)}, u32[]{:S(2)}) copy-start(bf16[1536,64]{0,1:T(8,128)(2,1)} %param.18) | copy-start | bytes 589828
  7.2 2.5 %copy-start.2 = (bf16[1,256,1536]{2,1,0:T(8,128)(2,1)S(1)}, bf16[1,256,1536]{2,1,0:T(8,128)(2,1)}, u32[]{:S(2)}) copy-start(bf16[1,256,1536]{2,1,0:T(8,128)(2,1)} %param.12) | copy-start | bytes 2359300
  7.2 54.3 %all-gather.7.cloned.1.call-start = ((), (), s32[]{:S(2)}) async-start(), calls=%async_computation.1 | async-start | bytes 7962624 | tf_op jit(solution)/shard_map/all_gather | solution.py:132
  7.9 94.4 %all-gather.5.cloned.1.call-start = ((), (), s32[]{:S(2)}) async-start(), calls=%async_computation | async-start | bytes 5308416 | tf_op jit(solution)/shard_map/all_gather | solution.py:135
  8.7 161.8 %all-gather.9.cloned.1.call-start = ((), (), s32[]{:S(2)}) async-start(), calls=%async_computation.2 | async-start | bytes 1966080 | tf_op jit(solution)/shard_map/all_gather | solution.py:166
  66.7 2.4 %copy-start.8 = (s32[1,1,4]{2,1,0:T(1,128)S(1)}, s32[1,1,4]{2,1,0:T(1,128)}, u32[]{:S(2)}) copy-start(s32[1,1,4]{2,1,0:T(1,128)} %param.20) | copy-start | bytes 52
  66.7 2.4 %copy-start.4 = (bf16[1,154,1536]{2,1,0:T(8,128)(2,1)S(1)}, bf16[1,154,1536]{2,1,0:T(8,128)(2,1)}, u32[]{:S(2)}) copy-start(bf16[1,154,1536]{2,1,0:T(8,128)(2,1)} %param.13) | copy-start | bytes 1419268
  66.7 3.6 %copy-start.7 = (f32[1,16,8,128]{3,2,1,0:T(8,128)S(1)}, f32[1,16,8,128]{3,2,1,0:T(8,128)}, u32[]{:S(2)}) copy-start(f32[1,16,8,128]{3,2,1,0:T(8,128)} %param.22) | copy-start | bytes 196612
  67.7 123.2 %all-gather.11.cloned.1.call-start = ((), (), s32[]{:S(2)}) async-start(), calls=%async_computation.3 | async-start | bytes 2654208 | tf_op jit(solution)/shard_map/all_gather | solution.py:179
  106.4 18.4 %collective-permute-start = (bf16[256,768]{1,0:T(8,128)(2,1)}, bf16[256,768]{1,0:T(8,128)(2,1)}, u32[]{:S(2)}, u32[]{:S(2)}) collective-permute-start(bf16[256,768]{1,0:T(8,128)(2,1)} %get-tuple-element.28), channel_id=1, source_target_pairs={{0,1},{1,2},{2,3},{3,0},{4,5},{5,6},{6,7},{7,4},{8,9},{9,10},{10,1... | collective-permute-start | bytes 1179656 | tf_op jit(solution)/shard_map/ppermute | solution.py:156
  109.8 39.9 %collective-permute-start.1 = (bf16[256,768]{1,0:T(8,128)(2,1)}, bf16[256,768]{1,0:T(8,128)(2,1)}, u32[]{:S(2)}, u32[]{:S(2)}) collective-permute-start(bf16[256,768]{1,0:T(8,128)(2,1)} %get-tuple-element.28), channel_id=1, source_target_pairs={{0,3},{1,0},{2,1},{3,2},{4,7},{5,4},{6,5},{7,6},{8,11},{9,8},{10,9... | collective-permute-start | bytes 1179656 | tf_op jit(solution)/shard_map/ppermute | solution.py:161
  124.8 33.1 %collective-permute-start.2 = (bf16[256,768]{1,0:T(8,128)(2,1)}, bf16[256,768]{1,0:T(8,128)(2,1)}, u32[]{:S(2)}, u32[]{:S(2)}) collective-permute-start(bf16[256,768]{1,0:T(8,128)(2,1)} %collective-permute-done), channel_id=1, source_target_pairs={{0,1},{1,2},{2,3},{3,0},{4,5},{5,6},{6,7},{7,4},{8,9},{9,10},{10,1... | collective-permute-start | bytes 1179656 | tf_op jit(solution)/shard_map/ppermute | solution.py:156
  165.8 4.6 %copy-start.1 = (f32[12,1024,256]{2,1,0:T(8,128)}, f32[12,1024,256]{2,1,0:T(8,128)S(1)}, u32[]{:S(2)}) copy-start(f32[12,1024,256]{2,1,0:T(8,128)S(1)} %get-tuple-element.45) | copy-start | bytes 37748740
  173.0 7.8 %copy-start.5 = (bf16[154,768]{0,1:T(8,128)(2,1)S(1)}, bf16[154,768]{0,1:T(8,128)(2,1)}, u32[]{:S(2)}) copy-start(bf16[154,768]{0,1:T(8,128)(2,1)} %copy.68) | copy-start | bytes 709636
  193.5 1.2 copy-start.3
  194.7 9.8 %copy-start.6 = (bf16[512,144]{0,1:T(8,128)(2,1)S(1)}, bf16[512,144]{0,1:T(8,128)(2,1)}, u32[]{:S(2)}) copy-start(bf16[512,144]{0,1:T(8,128)(2,1)} %param.23) | copy-start | bytes 442372
  194.8 6.4 %collective-permute-start.3 = (bf16[1,16,1,128]{1,3,2,0:T(8,128)(2,1)S(1)}, bf16[1,16,1,128]{1,3,2,0:T(8,128)(2,1)S(1)}, u32[]{:S(2)}, u32[]{:S(2)}) collective-permute-start(bf16[1,16,1,128]{1,3,2,0:T(8,128)(2,1)S(1)} %get-tuple-element.31), channel_id=1, source_target_pairs={{0,1},{1,2},{2,3},{4,5},{5,6},{6,7},{8,9},{9,10},{10,11},{12,13},{... | collective-permute-start | bytes 12296 | tf_op jit(solution)/shard_map/ppermute | solution.py:24
  198.2 5.8 %collective-permute-start.4 = (bf16[1,16,1,128]{1,3,2,0:T(8,128)(2,1)S(1)}, bf16[1,16,1,128]{1,3,2,0:T(8,128)(2,1)S(1)}, u32[]{:S(2)}, u32[]{:S(2)}) collective-permute-start(bf16[1,16,1,128]{1,3,2,0:T(8,128)(2,1)S(1)} %get-tuple-element.32), channel_id=1, source_target_pairs={{1,0},{2,1},{3,2},{5,4},{6,5},{7,6},{9,8},{10,9},{11,10},{13,12},{... | collective-permute-start | bytes 12296 | tf_op jit(solution)/shard_map/ppermute | solution.py:27
Sparse Core Ops, SparseCore 0:
  9.9 51.5 all-gather.6
  63.4 38.9 all-gather.4
  103.9 58.2 all-gather.8
  164.0 26.8 all-gather.10
